TPU v7x, 32 devices: a whole 2x2x4 slice. The times are simulated.
32 devices in a mesh: grp: 2 (over x), row: 16 (over z, y, core).
Axes of the slice: x: 2, y: 2, z: 4, core: 2. Of those that a mesh axis runs over, the one named last changes fastest.
Arguments:
- pair_rep: bfloat16 [64, 32, 128], P(('grp', 'row')), parts along dimension 0, may hold values from -6 to 6
- residue_mask: int32 [64], P('grp'), parts along dimension 0, may hold values 0 or 1
- side_weights: bfloat16 [2, 5, 128, 128], replicated, may hold values from -0.5 to 0.5
- out_weights: bfloat16 [2, 128, 128], replicated, may hold values from -0.5 to 0.5
- norm_gains: float32 [2, 2, 128], replicated, may hold values from 0.1 to 1.9
Outputs:
- updated: bfloat16 [64, 32, 128], P(('grp', 'row')), parts along dimension 0
There are 2 independent parts, one for each index of `grp`. A program takes and returns all parts, laid end to end along the dimension named above; an argument that names none is the same for every part. Nothing has to cross between parts.
All inputs are finite; a program needn't handle non-finite values.
Results may differ from a plain program's by a relative error of at most 0.013.
Values may be sent and summed in bfloat16 or wider, within the bound.
A program may use at most 64 MiB of HBM per device.

v0:
```python
import jax
import jax.numpy as jnp
from jax import lax
from jax.sharding import PartitionSpec as P


def layer_norm(values, gain, axis):
    centered = values - jnp.mean(values, axis=axis, keepdims=True)
    variance = jnp.mean(centered * centered, axis=axis, keepdims=True)
    return centered * lax.rsqrt(variance + 1e-05) * gain


def one_side(normed, gate_weight, value_weight, pair_mask):
    both_weights = jnp.stack([gate_weight, value_weight])
    sides = jnp.einsum("rnd,qde->qern", normed, both_weights, preferred_element_type=jnp.float32)
    return (jax.nn.sigmoid(sides[0]) * sides[1] * pair_mask[None]).astype(jnp.bfloat16)


def send_sides(normed, weights, pair_mask):
    left_proj = one_side(normed, weights[0], weights[1], pair_mask)
    left_cols = lax.all_to_all(left_proj, "row", split_axis=0, concat_axis=1, tiled=True)
    right_proj = one_side(normed, weights[2], weights[3], pair_mask)
    right_cols = lax.all_to_all(right_proj, "row", split_axis=0, concat_axis=1, tiled=True)
    return (left_cols, right_cols)


def one_update(pair_now, pair_mask, weights, out_weight, gains, incoming):
    pair_f32 = pair_now.astype(jnp.float32)
    normed = layer_norm(pair_f32, gains[0], -1).astype(jnp.bfloat16)
    left_cols, right_cols = send_sides(normed, weights, pair_mask)
    gate_vals = jax.nn.sigmoid(
        jnp.einsum("rnd,de->rne", normed, weights[4], preferred_element_type=jnp.float32)
    )
    if incoming:
        triangle = jnp.einsum(
            "cki,ckj->cij", left_cols, right_cols, preferred_element_type=jnp.float32
        )
    else:
        triangle = jnp.einsum(
            "cik,cjk->cij", left_cols, right_cols, preferred_element_type=jnp.float32
        )
    own_rows = lax.all_to_all(
        triangle.astype(jnp.bfloat16), "row", split_axis=1, concat_axis=0, tiled=True
    ).astype(triangle.dtype)
    tri_normed = layer_norm(own_rows, gains[1][:, None, None], 0).astype(jnp.bfloat16)
    projected = jnp.einsum(
        "crn,ce->rne", tri_normed, out_weight, preferred_element_type=jnp.float32
    )
    return (pair_f32 + gate_vals * projected).astype(jnp.bfloat16)


def body(pair_rep, residue_mask, side_weights, out_weights, norm_gains):
    row_count = pair_rep.shape[0]
    first_row = lax.axis_index("row") * row_count
    mask_f32 = residue_mask.astype(jnp.float32)
    own_mask = lax.dynamic_slice_in_dim(mask_f32, first_row, row_count, 0)
    pair_mask = own_mask[:, None] * mask_f32[None, :]
    middle = one_update(pair_rep, pair_mask, side_weights[0], out_weights[0], norm_gains[0], False)
    return one_update(middle, pair_mask, side_weights[1], out_weights[1], norm_gains[1], True)


def solution(mesh):
    in_specs = (P(("grp", "row"), None, None), P("grp"), P(), P(), P())
    out_specs = P(("grp", "row"), None, None)
    return jax.shard_map(body, mesh=mesh, in_specs=in_specs, out_specs=out_specs, check_vma=False)
```

profile of v0, /device:TPU:0, one launch (start us, length us, event | category | flops | bytes accessed | tf_op | source)
XLA Modules:
  0.0 73.9 jit_solution(7977564295664305855)
XLA Ops:
  0.0 0.9 %slice_bitcast_fusion.3 = (bf16[1,128,128]{2,1,0:T(8,128)(2,1)S(1)}, bf16[1,128,128]{2,1,0:T(8,128)(2,1)S(1)}, bf16[1,128,128]{2,1,0:T(8,128)(2,1)S(1)}, bf16[1,...) fusion(bf16[2,5,128,128]{3,2,1,0:T(8,128)(2,1)} %param.7), kind=kLoop, calls=%fused_computation.101 | loop fusion | bytes 524288 | tf_op jit(solution)/shard_map/slice | solution.py:20
  0.9 0.1 convert_reduce_fusion
  1.0 0.2 fusion.36
  1.2 0.7 copy-done.1
  1.9 0.6 copy-done.3
  2.7 0.2 fusion.15
  2.9 0.2 fusion.18
  3.2 0.1 copy.27
  3.3 0.7 reshape.159
  4.0 7.4 %all-to-all-start = ((bf16[16,2,256]{2,1,0:T(2,128)(2,1)}), bf16[16,2,256]{2,1,0:T(2,128)(2,1)S(1)}, u32[]{:S(2)}, u32[]{:S(2)}) async-start(bf16[16,2,256]{2,1,0:T(2,128)(2,1)} %reshape.159), calls=%async_computation | async-start | bytes 32768 | tf_op jit(solution)/shard_map/all_to_all | solution.py:21
  11.4 0.1 copy.30
  11.5 0.7 reshape.161
  12.2 5.7 %all-to-all-done = bf16[16,2,256]{2,1,0:T(2,128)(2,1)S(1)} async-done(((bf16[16,2,256]{2,1,0:T(2,128)(2,1)}), bf16[16,2,256]{2,1,0:T(2,128)(2,1)S(1)}, u32[]{:S(2)}, u32[]{:S(2)}) %all-to-all-start) | async-done | bytes 16416 | tf_op jit(solution)/shard_map/all_to_all | solution.py:21
  17.9 3.5 %all-to-all-start.1 = ((bf16[16,2,256]{2,1,0:T(2,128)(2,1)}), bf16[16,2,256]{2,1,0:T(2,128)(2,1)S(1)}, u32[]{:S(2)}, u32[]{:S(2)}) async-start(bf16[16,2,256]{2,1,0:T(2,128)(2,1)} %reshape.161), calls=%async_computation.1 | async-start | bytes 32768 | tf_op jit(solution)/shard_map/all_to_all | solution.py:23
  21.4 0.1 reshape.160
  21.6 6.3 %all-to-all-done.1 = bf16[16,2,256]{2,1,0:T(2,128)(2,1)S(1)} async-done(((bf16[16,2,256]{2,1,0:T(2,128)(2,1)}), bf16[16,2,256]{2,1,0:T(2,128)(2,1)S(1)}, u32[]{:S(2)}, u32[]{:S(2)}) %all-to-all-start.1) | async-done | bytes 16416 | tf_op jit(solution)/shard_map/all_to_all | solution.py:23
  27.9 0.1 reshape.162
  28.1 0.1 convolution_convert_fusion.1
  28.3 0.7 reshape.163
  29.0 3.5 %all-to-all-start.2 = ((bf16[16,2,256]{2,1,0:T(2,128)(2,1)}), bf16[16,2,256]{2,1,0:T(2,128)(2,1)S(1)}, u32[]{:S(2)}, u32[]{:S(2)}) async-start(bf16[16,2,256]{2,1,0:T(2,128)(2,1)} %reshape.163), calls=%async_computation.2 | async-start | bytes 32768 | tf_op jit(solution)/shard_map/all_to_all | solution.py:42
  32.5 1.0 %fusion.7 = f32[2,32,128]{2,1,0:T(8,128)S(1)} fusion(bf16[2,5,128,128]{3,2,1,0:T(8,128)(2,1)} %param.7, bf16[2,32,128]{2,1,0:T(8,128)(2,1)S(1)} %copy-done, f32[128]{0:T(128)S(1)} %get-tuple-element.16, f32[2,32]{1,0:T(2,128)S(1)} %add_rsqrt_fusion.3, f32[2,32]{1,0:T(2,128)S(1)} %broadcast_multiply_fusion.4), kind=kOutput, calls=%fused_computation.13 | convolution fusion | flops 2162688 | bytes 82944 | tf_op jit(solution)/shard_map/rnd,de->rne/dot_general | solution.py:32
  33.5 0.1 mul.172
  33.5 5.4 %all-to-all-done.2 = bf16[16,2,256]{2,1,0:T(2,128)(2,1)S(1)} async-done(((bf16[16,2,256]{2,1,0:T(2,128)(2,1)}), bf16[16,2,256]{2,1,0:T(2,128)(2,1)S(1)}, u32[]{:S(2)}, u32[]{:S(2)}) %all-to-all-start.2) | async-done | bytes 16416 | tf_op jit(solution)/shard_map/all_to_all | solution.py:42
  38.9 0.1 reshape.164
  39.2 0.8 %copy-done.2 = bf16[2,128,128]{2,1,0:T(8,128)(2,1)S(1)} copy-done((bf16[2,128,128]{2,1,0:T(8,128)(2,1)S(1)}, bf16[2,128,128]{2,1,0:T(8,128)(2,1)}, u32[]{:S(2)}) %copy-start.2) | copy-done | bytes 65560
  40.0 0.3 fusion.82
  40.3 0.2 multiply_reduce_fusion.2
  40.5 0.1 multiply_convert_fusion.2
  40.6 0.1 fusion.24
  40.7 0.1 fusion.21
  40.8 0.1 fusion.47
  40.9 0.1 copy.36
  41.0 0.7 reshape.167
  41.8 3.5 %all-to-all-start.3 = ((bf16[16,2,256]{2,1,0:T(2,128)(2,1)}), bf16[16,2,256]{2,1,0:T(2,128)(2,1)S(1)}, u32[]{:S(2)}, u32[]{:S(2)}) async-start(bf16[16,2,256]{2,1,0:T(2,128)(2,1)} %reshape.167), calls=%async_computation.3 | async-start | bytes 32768 | tf_op jit(solution)/shard_map/all_to_all | solution.py:21
  45.3 0.1 copy.39
  45.4 0.7 reshape.165
  46.1 5.6 %all-to-all-done.3 = bf16[16,2,256]{2,1,0:T(2,128)(2,1)S(1)} async-done(((bf16[16,2,256]{2,1,0:T(2,128)(2,1)}), bf16[16,2,256]{2,1,0:T(2,128)(2,1)S(1)}, u32[]{:S(2)}, u32[]{:S(2)}) %all-to-all-start.3) | async-done | bytes 16416 | tf_op jit(solution)/shard_map/all_to_all | solution.py:21
  51.7 3.5 %all-to-all-start.4 = ((bf16[16,2,256]{2,1,0:T(2,128)(2,1)}), bf16[16,2,256]{2,1,0:T(2,128)(2,1)S(1)}, u32[]{:S(2)}, u32[]{:S(2)}) async-start(bf16[16,2,256]{2,1,0:T(2,128)(2,1)} %reshape.165), calls=%async_computation.4 | async-start | bytes 32768 | tf_op jit(solution)/shard_map/all_to_all | solution.py:23
  55.3 0.1 reshape.168
  55.5 6.2 %all-to-all-done.4 = bf16[16,2,256]{2,1,0:T(2,128)(2,1)S(1)} async-done(((bf16[16,2,256]{2,1,0:T(2,128)(2,1)}), bf16[16,2,256]{2,1,0:T(2,128)(2,1)S(1)}, u32[]{:S(2)}, u32[]{:S(2)}) %all-to-all-start.4) | async-done | bytes 16416 | tf_op jit(solution)/shard_map/all_to_all | solution.py:23
  61.7 0.1 reshape.166
  61.9 0.2 convolution_convert_fusion
  62.1 0.7 reshape.169
  62.8 3.5 %all-to-all-start.5 = ((bf16[16,2,256]{2,1,0:T(2,128)(2,1)}), bf16[16,2,256]{2,1,0:T(2,128)(2,1)S(1)}, u32[]{:S(2)}, u32[]{:S(2)}) async-start(bf16[16,2,256]{2,1,0:T(2,128)(2,1)} %reshape.169), calls=%async_computation.5 | async-start | bytes 32768 | tf_op jit(solution)/shard_map/all_to_all | solution.py:42
  66.3 0.9 %fusion.3 = f32[2,32,128]{2,1,0:T(8,128)S(1)} fusion(bf16[2,32,128]{2,1,0:T(8,128)(2,1)S(1)} %multiply_convert_fusion.2, bf16[2,5,128,128]{3,2,1,0:T(8,128)(2,1)} %param.7), kind=kOutput, calls=%fused_computation.7 | convolution fusion | flops 2121728 | bytes 81920 | tf_op jit(solution)/shard_map/rnd,de->rne/dot_general | solution.py:32
  67.3 5.5 %all-to-all-done.5 = bf16[16,2,256]{2,1,0:T(2,128)(2,1)S(1)} async-done(((bf16[16,2,256]{2,1,0:T(2,128)(2,1)}), bf16[16,2,256]{2,1,0:T(2,128)(2,1)S(1)}, u32[]{:S(2)}, u32[]{:S(2)}) %all-to-all-start.5) | async-done | bytes 16416 | tf_op jit(solution)/shard_map/all_to_all | solution.py:42
  72.8 0.1 reshape.170
  73.0 0.9 %fusion.10 = bf16[2,32,128]{2,1,0:T(8,128)(2,1)} fusion(f32[2,32,128]{2,1,0:T(8,128)S(1)} %get-tuple-element.24, f32[2,32,128]{2,1,0:T(8,128)S(1)} %fusion.3, f32[16,8]{1,0:T(8,128)S(1)} %mul.189, f32[2,32]{1,0:T(2,128)S(1)} %add_rsqrt_fusion, f32[2,32]{1,0:T(2,128)S(1)} %broadcast_multiply_fusion.1, bf16[2,128,128]{2,1,0:T(8,128)(2,1)S(1)} %copy-done.2, ...), kind=kOutput, calls=%fused_computation.16 | convolution fusion | flops 2162688 | bytes 190464 | tf_op jit(solution)/shard_map/crn,ce->rne/dot_general | solution.py:46
  (35 shorter events, 0.9 us)
Async XLA Ops:
  0.0 0.9 %copy-start = (bf16[2,32,128]{2,1,0:T(8,128)(2,1)S(1)}, bf16[2,32,128]{2,1,0:T(8,128)(2,1)}, u32[]{:S(2)}) copy-start(bf16[2,32,128]{2,1,0:T(8,128)(2,1)} %param.5) | copy-start | bytes 49156
  1.2 0.7 copy-start.1
  1.9 0.7 copy-start.3
  4.0 13.9 %all-to-all-start = ((bf16[16,2,256]{2,1,0:T(2,128)(2,1)}), bf16[16,2,256]{2,1,0:T(2,128)(2,1)S(1)}, u32[]{:S(2)}, u32[]{:S(2)}) async-start(bf16[16,2,256]{2,1,0:T(2,128)(2,1)} %reshape.159), calls=%async_computation | async-start | bytes 32768 | tf_op jit(solution)/shard_map/all_to_all | solution.py:21
  17.9 10.0 %all-to-all-start.1 = ((bf16[16,2,256]{2,1,0:T(2,128)(2,1)}), bf16[16,2,256]{2,1,0:T(2,128)(2,1)S(1)}, u32[]{:S(2)}, u32[]{:S(2)}) async-start(bf16[16,2,256]{2,1,0:T(2,128)(2,1)} %reshape.161), calls=%async_computation.1 | async-start | bytes 32768 | tf_op jit(solution)/shard_map/all_to_all | solution.py:23
  29.0 10.0 %all-to-all-start.2 = ((bf16[16,2,256]{2,1,0:T(2,128)(2,1)}), bf16[16,2,256]{2,1,0:T(2,128)(2,1)S(1)}, u32[]{:S(2)}, u32[]{:S(2)}) async-start(bf16[16,2,256]{2,1,0:T(2,128)(2,1)} %reshape.163), calls=%async_computation.2 | async-start | bytes 32768 | tf_op jit(solution)/shard_map/all_to_all | solution.py:42
  39.1 0.8 %copy-start.2 = (bf16[2,128,128]{2,1,0:T(8,128)(2,1)S(1)}, bf16[2,128,128]{2,1,0:T(8,128)(2,1)}, u32[]{:S(2)}) copy-start(bf16[2,128,128]{2,1,0:T(8,128)(2,1)} %param.8) | copy-start | bytes 196612
  41.8 10.0 %all-to-all-start.3 = ((bf16[16,2,256]{2,1,0:T(2,128)(2,1)}), bf16[16,2,256]{2,1,0:T(2,128)(2,1)S(1)}, u32[]{:S(2)}, u32[]{:S(2)}) async-start(bf16[16,2,256]{2,1,0:T(2,128)(2,1)} %reshape.167), calls=%async_computation.3 | async-start | bytes 32768 | tf_op jit(solution)/shard_map/all_to_all | solution.py:21
  51.7 10.0 %all-to-all-start.4 = ((bf16[16,2,256]{2,1,0:T(2,128)(2,1)}), bf16[16,2,256]{2,1,0:T(2,128)(2,1)S(1)}, u32[]{:S(2)}, u32[]{:S(2)}) async-start(bf16[16,2,256]{2,1,0:T(2,128)(2,1)} %reshape.165), calls=%async_computation.4 | async-start | bytes 32768 | tf_op jit(solution)/shard_map/all_to_all | solution.py:23
  62.8 10.0 %all-to-all-start.5 = ((bf16[16,2,256]{2,1,0:T(2,128)(2,1)}), bf16[16,2,256]{2,1,0:T(2,128)(2,1)S(1)}, u32[]{:S(2)}, u32[]{:S(2)}) async-start(bf16[16,2,256]{2,1,0:T(2,128)(2,1)} %reshape.169), calls=%async_computation.5 | async-start | bytes 32768 | tf_op jit(solution)/shard_map/all_to_all | solution.py:42
where the time goes:
time: 74.6 us; the launch traced here: 73.9 us
  waiting for transfers between devices  34.7 us (47%)
  starting transfers between devices  24.9 us (33%)
  local copies, waits for them, and re-layouts  8.99 us (12%)
  matrix products  4.08 us (5%)
  other arithmetic  0.96 us (1%)
    all_to_all x2, waiting for transfers between devices, send_sides(): lax.all_to_all(right_proj, 'row', split_axis=0, concat_axis=1, tiled=True)  12.5 us
    all_to_all x2, waiting for transfers between devices, send_sides(): lax.all_to_all(left_proj, 'row', split_axis=0, concat_axis=1, tiled=True)  11.3 us
    all_to_all x2, waiting for transfers between devices, one_update(): lax.all_to_all(triangle.astype(jnp.bfloat16), 'row', split_axis=1, concat...  10.9 us
    all_to_all x2, starting transfers between devices, send_sides(): lax.all_to_all(left_proj, 'row', split_axis=0, concat_axis=1, tiled=True)  10.9 us
    unnamed x20, local copies, waits for them, and re-layouts  6.99 us
    all_to_all x2, starting transfers between devices, one_update(): lax.all_to_all(triangle.astype(jnp.bfloat16), 'row', split_axis=1, concat...  6.99 us
    all_to_all x2, starting transfers between devices, send_sides(): lax.all_to_all(right_proj, 'row', split_axis=0, concat_axis=1, tiled=True)  6.99 us
    dot_general x2, matrix products, one_update(): jnp.einsum('rnd,de->rne', normed, weights[4], preferred_element_type=jnp....  1.88 us
  transfers between devices with their start and end apart: 6, of which 6 were waited for; matrix products, arithmetic and copies ran while one was open for 5% of the time, Pallas kernels for 0%

commit v1 on v0

--- a/solution.py
+++ b/solution.py
@@ -1,7 +1,15 @@
+import functools
+
 import jax
 import jax.numpy as jnp
 from jax import lax
+from jax.experimental import pallas as pl
+from jax.experimental.pallas import tpu as pltpu
 from jax.sharding import PartitionSpec as P
+
+MESH = pl.DeviceIdType.MESH
+CHUNK = 256
+GROUP_BYTES = 1 << 20
 
 
 def layer_norm(values, gain, axis):
@@ -49,7 +57,7 @@
     return (pair_f32 + gate_vals * projected).astype(jnp.bfloat16)
 
 
-def body(pair_rep, residue_mask, side_weights, out_weights, norm_gains):
+def large_body(pair_rep, residue_mask, side_weights, out_weights, norm_gains):
     row_count = pair_rep.shape[0]
     first_row = lax.axis_index("row") * row_count
     mask_f32 = residue_mask.astype(jnp.float32)
@@ -59,7 +67,190 @@
     return one_update(middle, pair_mask, side_weights[1], out_weights[1], norm_gains[1], True)
 
 
+def sigmoid(values):
+    return 0.5 * jnp.tanh(0.5 * values) + 0.5
+
+
+def dot(a, b):
+    return jnp.dot(a, b, preferred_element_type=jnp.float32)
+
+
+def pair_kernel(
+    ranks, size, rows,
+    pair_ref, mask_ref, side_ref, out_ref, gain_ref, result_ref,
+    pair_all, side_w, out_w, gain_w, mask_w, mask_col, pair_mask,
+    left, right_t, gate, tri, pair_mid, normed_mid, right_mid,
+    send_sem, recv_sem, load_sem,
+):
+    chan = pair_all.shape[1]
+    block = rows * size
+    grp, me = lax.axis_index("grp"), lax.axis_index("row")
+    chips = ranks // 2
+    sibling = me + 1 - 2 * (me % 2)
+    peers = [(me + 2 * step) % ranks for step in range(1, chips)]
+
+    barrier = pltpu.get_barrier_semaphore()
+    for peer in peers + [sibling]:
+        pl.semaphore_signal(barrier, inc=1, device_id=(grp, peer), device_id_type=MESH)
+
+    def part(rank):
+        return pair_all.at[pl.ds(pl.multiple_of(rank * block, block), block)]
+
+    loads = [
+        pltpu.make_async_copy(source, target, load_sem.at[index])
+        for index, (source, target) in enumerate(
+            [(pair_ref, part(me)), (mask_ref, mask_w), (side_ref, side_w), (out_ref, out_w), (gain_ref, gain_w)]
+        )
+    ]
+    for load in loads:
+        load.start()
+
+    loads[1].wait()
+    at_row = lax.broadcasted_iota(jnp.int32, (size, size), 0)
+    at_col = lax.broadcasted_iota(jnp.int32, (size, size), 1)
+    mask_row = jnp.broadcast_to(mask_w[...].astype(jnp.float32), (size, size))
+    column = jnp.sum(jnp.where(at_row == at_col, mask_row, 0.0), axis=1, keepdims=True)
+    mask_col[...] = jnp.broadcast_to(column, (size, chan))
+
+    pl.semaphore_wait(barrier, chips)
+
+    copies = []
+
+    def put(source, rank, target):
+        copy = pltpu.make_async_remote_copy(
+            src_ref=source, dst_ref=part(rank), send_sem=send_sem.at[len(copies)],
+            recv_sem=recv_sem.at[rank], device_id=(grp, target), device_id_type=MESH,
+        )
+        copy.start()
+        copies.append(copy)
+
+    def arrive(rank):
+        pltpu.make_async_remote_copy(
+            src_ref=part(rank), dst_ref=part(rank), send_sem=send_sem.at[0],
+            recv_sem=recv_sem.at[rank], device_id=(grp, sibling), device_id_type=MESH,
+        ).wait_recv()
+
+    for peer in peers + [sibling]:
+        put(pair_ref, me, peer)
+
+    def fill_mask(first, carry):
+        mask_one = mask_col[pl.ds(first, 1), :]
+        pair_mask[pl.ds(pl.multiple_of(first * size, size), size), :] = mask_one * mask_col[...]
+        return carry
+
+    lax.fori_loop(0, size, fill_mask, 0)
+
+    for peer in peers:
+        arrive(peer)
+        put(part(peer), peer, sibling)
+    for load in (loads[0], loads[2], loads[3], loads[4]):
+        load.wait()
+    for step in range(chips):
+        arrive((sibling + 2 * step) % ranks)
+
+    gains = [[gain_w[u, pl.ds(q, 1), :] for q in range(2)] for u in range(2)]
+
+    def project(step, carry):
+        span = pl.ds(pl.multiple_of(step * CHUNK, CHUNK), CHUNK)
+        normed = layer_norm(pair_all[span, :].astype(jnp.float32), gains[0][0], -1).astype(jnp.bfloat16)
+        mask = pair_mask[span, :]
+        lefts = dot(normed, jnp.concatenate([side_w[0, 0], side_w[0, 1]], axis=1))
+        left[span, :] = (sigmoid(lefts[:, :chan]) * lefts[:, chan:] * mask).astype(jnp.bfloat16).astype(jnp.float32)
+        rights = dot(normed, jnp.concatenate([side_w[0, 2], side_w[0, 3]], axis=1))
+        right = (sigmoid(rights[:, :chan]) * rights[:, chan:] * mask).astype(jnp.bfloat16).astype(jnp.float32)
+        for index in range(CHUNK // size):
+            right_t[pl.ds(step * (CHUNK // size) + index, size, stride=size), :] = right[index * size:(index + 1) * size]
+        gate[span, :] = sigmoid(dot(normed, side_w[0, 4]))
+        return carry
+
+    lax.fori_loop(0, size * size // CHUNK, project, 0)
+
+    def outgoing(step, carry):
+        first = pl.multiple_of(step * 4 * size, 4 * size)
+        sums = [jnp.zeros((size, chan), jnp.float32) for _ in range(4)]
+        for k in range(size):
+            rights = right_t[k * size:(k + 1) * size, :]
+            for index in range(4):
+                sums[index] += left[pl.ds(first + index * size + k, 1), :] * rights
+        for index in range(4):
+            tri[pl.ds(pl.multiple_of(first + index * size, size), size), :] = sums[index]
+        return carry
+
+    lax.fori_loop(0, size // 4, outgoing, 0)
+
+    def finish(step, carry):
+        span = pl.ds(pl.multiple_of(step * CHUNK, CHUNK), CHUNK)
+        tri_normed = layer_norm(tri[span, :], gains[0][1], -1).astype(jnp.bfloat16)
+        middle = pair_all[span, :].astype(jnp.float32) + gate[span, :] * dot(tri_normed, out_w[0])
+        middle = middle.astype(jnp.bfloat16).astype(jnp.float32)
+        pair_mid[span, :] = middle
+        normed = layer_norm(middle, gains[1][0], -1).astype(jnp.bfloat16)
+        normed_mid[span, :] = normed.astype(jnp.float32)
+        rights = dot(normed, jnp.concatenate([side_w[1, 2], side_w[1, 3]], axis=1))
+        right = sigmoid(rights[:, :chan]) * rights[:, chan:] * pair_mask[span, :]
+        right_mid[span, :] = right.astype(jnp.bfloat16).astype(jnp.float32)
+        return carry
+
+    lax.fori_loop(0, size * size // CHUNK, finish, 0)
+
+    own = pl.ds(pl.multiple_of(me * block, block), block)
+    columns = jnp.concatenate(
+        [normed_mid[pl.ds(me * rows + index, size, stride=size), :] for index in range(rows)], axis=0
+    ).astype(jnp.bfloat16)
+    lefts = dot(columns, jnp.concatenate([side_w[1, 0], side_w[1, 1]], axis=1))
+    left_own = sigmoid(lefts[:, :chan]) * lefts[:, chan:] * pair_mask[own, :]
+    left_own = left_own.astype(jnp.bfloat16).astype(jnp.float32)
+    gate_own = sigmoid(dot(normed_mid[own, :].astype(jnp.bfloat16), side_w[1, 4]))
+    sums = [jnp.zeros((size, chan), jnp.float32) for _ in range(rows)]
+    for k in range(size):
+        rights = right_mid[k * size:(k + 1) * size, :]
+        for index in range(rows):
+            sums[index] += left_own[index * size + k:index * size + k + 1] * rights
+    tri_normed = layer_norm(jnp.concatenate(sums, axis=0), gains[1][1], -1).astype(jnp.bfloat16)
+    result_ref[...] = (pair_mid[own, :] + gate_own * dot(tri_normed, out_w[1])).astype(jnp.bfloat16)
+
+    for copy in copies:
+        copy.wait_send()
+
+
+def group_body(ranks, pair_rep, residue_mask, side_weights, out_weights, norm_gains):
+    rows, size, chan = pair_rep.shape
+    pairs = size * size
+    wide = pltpu.VMEM((pairs, chan), jnp.float32)
+    result = pl.pallas_call(
+        functools.partial(pair_kernel, ranks, size, rows),
+        out_shape=jax.ShapeDtypeStruct((rows * size, chan), jnp.bfloat16),
+        in_specs=[pl.BlockSpec(memory_space=pl.ANY)] * 5,
+        out_specs=pl.BlockSpec(memory_space=pltpu.VMEM),
+        scratch_shapes=[
+            pltpu.VMEM((pairs, chan), jnp.bfloat16),
+            pltpu.VMEM(side_weights.shape, jnp.bfloat16),
+            pltpu.VMEM(out_weights.shape, jnp.bfloat16),
+            pltpu.VMEM(norm_gains.shape, jnp.float32),
+            pltpu.VMEM((1, size), jnp.int32),
+            pltpu.VMEM((size, chan), jnp.float32),
+            wide, wide, wide, wide, wide, wide, wide, wide,
+            pltpu.SemaphoreType.DMA((ranks,)),
+            pltpu.SemaphoreType.DMA((ranks,)),
+            pltpu.SemaphoreType.DMA((5,)),
+        ],
+        compiler_params=pltpu.CompilerParams(
+            collective_id=0, has_side_effects=True, vmem_limit_bytes=32 << 20
+        ),
+    )(pair_rep.reshape(rows * size, chan), residue_mask.reshape(1, size), side_weights, out_weights, norm_gains)
+    return result.reshape(pair_rep.shape)
+
+
+def body(ranks, pair_rep, residue_mask, side_weights, out_weights, norm_gains):
+    rows, size, chan = pair_rep.shape
+    fits = size * size * chan * 4 <= GROUP_BYTES and size * size % CHUNK == 0 and CHUNK % size == 0
+    if fits and ranks % 2 == 0 and ranks > 2:
+        return group_body(ranks, pair_rep, residue_mask, side_weights, out_weights, norm_gains)
+    return large_body(pair_rep, residue_mask, side_weights, out_weights, norm_gains)
+
+
 def solution(mesh):
     in_specs = (P(("grp", "row"), None, None), P("grp"), P(), P(), P())
     out_specs = P(("grp", "row"), None, None)
-    return jax.shard_map(body, mesh=mesh, in_specs=in_specs, out_specs=out_specs, check_vma=False)
+    mapped = functools.partial(body, mesh.shape["row"])
+    return jax.shard_map(mapped, mesh=mesh, in_specs=in_specs, out_specs=out_specs, check_vma=False)

time: 74.6 us -> 21 us (0.28)
  the two profiles are of different devices: /device:TPU:0 before, /device:TPU:1 now
where the time goes in v1:
time: 21 us; the launch traced here: 20.7 us
  Pallas kernels  16.9 us (80%)
  local copies, waits for them, and re-layouts  3.82 us (18%)
    pallas_call x1, Pallas kernels, group_body(): pl.pallas_call(functools.partial(pair_kernel, ranks, size, rows), out_sha...  16.9 us
    unnamed x11, local copies, waits for them, and re-layouts  3.82 us

profile of v1, /device:TPU:1, one launch (start us, length us, event | category | flops | bytes accessed | tf_op | source)
XLA Modules:
  0.0 20.7 jit_solution(15893346738698353906)
XLA Ops:
  0.0 0.0 copy-start.3
  0.0 0.0 copy-start.4
  0.0 0.7 %copy-done.3 = f32[2,2,128]{2,1,0:T(2,128)S(1)} copy-done((f32[2,2,128]{2,1,0:T(2,128)S(1)}, f32[2,2,128]{2,1,0:T(2,128)}, u32[]{:S(2)}) %copy-start.3) | copy-done | bytes 2072
  0.7 0.0 copy-done.4
  0.7 0.0 copy-start
  0.7 1.0 %copy-done = bf16[2,5,128,128]{3,2,1,0:T(8,128)(2,1)S(1)} copy-done((bf16[2,5,128,128]{3,2,1,0:T(8,128)(2,1)S(1)}, bf16[2,5,128,128]{3,2,1,0:T(8,128)(2,1)}, u32[]{:S(2)}) %copy-start) | copy-done | bytes 327704
  1.7 0.0 copy-start.1
  1.7 0.8 %copy-done.1 = bf16[2,128,128]{2,1,0:T(8,128)(2,1)S(1)} copy-done((bf16[2,128,128]{2,1,0:T(8,128)(2,1)S(1)}, bf16[2,128,128]{2,1,0:T(8,128)(2,1)}, u32[]{:S(2)}) %copy-start.1) | copy-done | bytes 65560
  2.5 0.0 copy-start.2
  2.5 0.7 %copy-done.2 = bf16[2,32,128]{2,1,0:T(8,128)(2,1)S(1)} copy-done((bf16[2,32,128]{2,1,0:T(8,128)(2,1)S(1)}, bf16[2,32,128]{2,1,0:T(8,128)(2,1)}, u32[]{:S(2)}) %copy-start.2) | copy-done | bytes 16408
  3.2 16.9 %shard_map.55 = bf16[64,128]{1,0:T(8,128)(2,1)S(1)} custom-call(bf16[64,128]{1,0:T(8,128)(2,1)S(1)} %bitcast.4, s32[1,32]{1,0:T(1,128)S(1)} %bitcast.5, bf16[2,5,128,128]{3,2,1,0:T(8,128)(2,1)S(1)} %copy-done, bf16[2,128,128]{2,1,0:T(8,128)(2,1)S(1)} %copy-done.1, f32[2,2,128]{2,1,0:T(2,128)S(1)} %copy-done.3), custom_call_target="tpu_custom_call" | custom-call | tf_op jit(solution)/shard_map/pallas_call | solution.py:220
  20.1 0.6 %copy.7 = bf16[2,32,128]{2,1,0:T(8,128)(2,1)} copy(bf16[2,32,128]{2,1,0:T(8,128)(2,1)S(1)} %bitcast.3) | data formatting | bytes 32768
Async XLA Ops:
  0.0 0.7 %copy-start.3 = (f32[2,2,128]{2,1,0:T(2,128)S(1)}, f32[2,2,128]{2,1,0:T(2,128)}, u32[]{:S(2)}) copy-start(f32[2,2,128]{2,1,0:T(2,128)} %gain_ref.1) | copy-start | bytes 6148
  0.0 0.7 %copy-start.4 = (s32[32]{0:T(128)S(1)}, s32[32]{0:T(128)}, u32[]{:S(2)}) copy-start(s32[32]{0:T(128)} %param.6) | copy-start | bytes 388
  0.7 1.0 %copy-start = (bf16[2,5,128,128]{3,2,1,0:T(8,128)(2,1)S(1)}, bf16[2,5,128,128]{3,2,1,0:T(8,128)(2,1)}, u32[]{:S(2)}) copy-start(bf16[2,5,128,128]{3,2,1,0:T(8,128)(2,1)} %side_ref.1) | copy-start | bytes 983044
  1.7 0.8 %copy-start.1 = (bf16[2,128,128]{2,1,0:T(8,128)(2,1)S(1)}, bf16[2,128,128]{2,1,0:T(8,128)(2,1)}, u32[]{:S(2)}) copy-start(bf16[2,128,128]{2,1,0:T(8,128)(2,1)} %out_ref.1) | copy-start | bytes 196612
  2.5 0.7 %copy-start.2 = (bf16[2,32,128]{2,1,0:T(8,128)(2,1)S(1)}, bf16[2,32,128]{2,1,0:T(8,128)(2,1)}, u32[]{:S(2)}) copy-start(bf16[2,32,128]{2,1,0:T(8,128)(2,1)} %param.5) | copy-start | bytes 49156

commit v2 on v1

--- a/solution.py
+++ b/solution.py
@@ -220,7 +220,7 @@
     result = pl.pallas_call(
         functools.partial(pair_kernel, ranks, size, rows),
         out_shape=jax.ShapeDtypeStruct((rows * size, chan), jnp.bfloat16),
-        in_specs=[pl.BlockSpec(memory_space=pl.ANY)] * 5,
+        in_specs=[pl.BlockSpec(memory_space=pltpu.HBM)] * 5,
         out_specs=pl.BlockSpec(memory_space=pltpu.VMEM),
         scratch_shapes=[
             pltpu.VMEM((pairs, chan), jnp.bfloat16),

time: 21 us -> 21 us (level)
  no operation moved by 1% of the time
where the time goes in v2:
time: 21 us; the launch traced here: 20.7 us
  Pallas kernels  16.9 us (80%)
  local copies, waits for them, and re-layouts  3.82 us (18%)
    pallas_call x1, Pallas kernels, group_body(): pl.pallas_call(functools.partial(pair_kernel, ranks, size, rows), out_sha...  16.9 us
    unnamed x11, local copies, waits for them, and re-layouts  3.82 us

profile of v2, /device:TPU:1, one launch (start us, length us, event | category | flops | bytes accessed | tf_op | source)
XLA Modules:
  0.0 20.7 jit_solution(15893346738698353906)
XLA Ops:
  0.0 0.0 copy-start.3
  0.0 0.0 copy-start.4
  0.0 0.7 %copy-done.3 = f32[2,2,128]{2,1,0:T(2,128)S(1)} copy-done((f32[2,2,128]{2,1,0:T(2,128)S(1)}, f32[2,2,128]{2,1,0:T(2,128)}, u32[]{:S(2)}) %copy-start.3) | copy-done | bytes 2072
  0.7 0.0 copy-done.4
  0.7 0.0 copy-start
  0.7 1.0 %copy-done = bf16[2,5,128,128]{3,2,1,0:T(8,128)(2,1)S(1)} copy-done((bf16[2,5,128,128]{3,2,1,0:T(8,128)(2,1)S(1)}, bf16[2,5,128,128]{3,2,1,0:T(8,128)(2,1)}, u32[]{:S(2)}) %copy-start) | copy-done | bytes 327704
  1.7 0.0 copy-start.1
  1.7 0.8 %copy-done.1 = bf16[2,128,128]{2,1,0:T(8,128)(2,1)S(1)} copy-done((bf16[2,128,128]{2,1,0:T(8,128)(2,1)S(1)}, bf16[2,128,128]{2,1,0:T(8,128)(2,1)}, u32[]{:S(2)}) %copy-start.1) | copy-done | bytes 65560
  2.5 0.0 copy-start.2
  2.5 0.7 %copy-done.2 = bf16[2,32,128]{2,1,0:T(8,128)(2,1)S(1)} copy-done((bf16[2,32,128]{2,1,0:T(8,128)(2,1)S(1)}, bf16[2,32,128]{2,1,0:T(8,128)(2,1)}, u32[]{:S(2)}) %copy-start.2) | copy-done | bytes 16408
  3.2 16.9 %shard_map.55 = bf16[64,128]{1,0:T(8,128)(2,1)S(1)} custom-call(bf16[64,128]{1,0:T(8,128)(2,1)S(1)} %bitcast.4, s32[1,32]{1,0:T(1,128)S(1)} %bitcast.5, bf16[2,5,128,128]{3,2,1,0:T(8,128)(2,1)S(1)} %copy-done, bf16[2,128,128]{2,1,0:T(8,128)(2,1)S(1)} %copy-done.1, f32[2,2,128]{2,1,0:T(2,128)S(1)} %copy-done.3), custom_call_target="tpu_custom_call" | custom-call | tf_op jit(solution)/shard_map/pallas_call | solution.py:220
  20.1 0.6 %copy.7 = bf16[2,32,128]{2,1,0:T(8,128)(2,1)} copy(bf16[2,32,128]{2,1,0:T(8,128)(2,1)S(1)} %bitcast.3) | data formatting | bytes 32768
Async XLA Ops:
  0.0 0.7 %copy-start.3 = (f32[2,2,128]{2,1,0:T(2,128)S(1)}, f32[2,2,128]{2,1,0:T(2,128)}, u32[]{:S(2)}) copy-start(f32[2,2,128]{2,1,0:T(2,128)} %gain_ref.1) | copy-start | bytes 6148
  0.0 0.7 %copy-start.4 = (s32[32]{0:T(128)S(1)}, s32[32]{0:T(128)}, u32[]{:S(2)}) copy-start(s32[32]{0:T(128)} %param.6) | copy-start | bytes 388
  0.7 1.0 %copy-start = (bf16[2,5,128,128]{3,2,1,0:T(8,128)(2,1)S(1)}, bf16[2,5,128,128]{3,2,1,0:T(8,128)(2,1)}, u32[]{:S(2)}) copy-start(bf16[2,5,128,128]{3,2,1,0:T(8,128)(2,1)} %side_ref.1) | copy-start | bytes 983044
  1.7 0.8 %copy-start.1 = (bf16[2,128,128]{2,1,0:T(8,128)(2,1)S(1)}, bf16[2,128,128]{2,1,0:T(8,128)(2,1)}, u32[]{:S(2)}) copy-start(bf16[2,128,128]{2,1,0:T(8,128)(2,1)} %out_ref.1) | copy-start | bytes 196612
  2.5 0.7 %copy-start.2 = (bf16[2,32,128]{2,1,0:T(8,128)(2,1)S(1)}, bf16[2,32,128]{2,1,0:T(8,128)(2,1)}, u32[]{:S(2)}) copy-start(bf16[2,32,128]{2,1,0:T(8,128)(2,1)} %param.5) | copy-start | bytes 49156

commit v3 on v2

--- a/solution.py
+++ b/solution.py
@@ -219,7 +219,7 @@
     wide = pltpu.VMEM((pairs, chan), jnp.float32)
     result = pl.pallas_call(
         functools.partial(pair_kernel, ranks, size, rows),
-        out_shape=jax.ShapeDtypeStruct((rows * size, chan), jnp.bfloat16),
+        out_shape=pltpu.VMEM((rows * size, chan), jnp.bfloat16),
         in_specs=[pl.BlockSpec(memory_space=pltpu.HBM)] * 5,
         out_specs=pl.BlockSpec(memory_space=pltpu.VMEM),
         scratch_shapes=[
@@ -235,7 +235,7 @@
             pltpu.SemaphoreType.DMA((5,)),
         ],
         compiler_params=pltpu.CompilerParams(
-            collective_id=0, has_side_effects=True, vmem_limit_bytes=32 << 20
+            collective_id=0, has_side_effects=True, vmem_limit_bytes=60 << 20
         ),
     )(pair_rep.reshape(rows * size, chan), residue_mask.reshape(1, size), side_weights, out_weights, norm_gains)
     return result.reshape(pair_rep.shape)

time: 21 us -> 17.9 us (0.85)
  local copies, waits for them, and re-layouts: 3.82 us -> 0.61 us
  Pallas kernels: 16.9 us -> 17.2 us
    unnamed x11 -> x1, local copies, waits for them, and re-layouts: 3.82 us -> 0.61 us
    pallas_call x1, Pallas kernels: 16.9 us -> 17.2 us  [group_body(): pl.pallas_call(functools.partial(pair_kernel, ranks, size, rows), out_sha...]
where the time goes in v3:
time: 17.9 us; the launch traced here: 17.8 us
  Pallas kernels  17.2 us (96%)
  local copies, waits for them, and re-layouts  0.61 us (3%)
    pallas_call x1, Pallas kernels, group_body(): pl.pallas_call(functools.partial(pair_kernel, ranks, size, rows), out_sha...  17.2 us
    unnamed x1, local copies, waits for them, and re-layouts  0.61 us

profile of v3, /device:TPU:1, one launch (start us, length us, event | category | flops | bytes accessed | tf_op | source)
XLA Modules:
  0.0 17.8 jit_solution(6134002947391395952)
XLA Ops:
  0.0 17.2 %shard_map.55 = bf16[64,128]{1,0:T(8,128)(2,1)S(1)} custom-call(bf16[64,128]{1,0:T(8,128)(2,1)} %bitcast.4, s32[1,32]{1,0:T(1,128)} %bitcast.5, bf16[2,5,128,128]{3,2,1,0:T(8,128)(2,1)} %side_ref.1, bf16[2,128,128]{2,1,0:T(8,128)(2,1)} %out_ref.1, f32[2,2,128]{2,1,0:T(2,128)} %gain_ref.1), custom_call_target="tpu_custom_call" | custom-call | tf_op jit(solution)/shard_map/pallas_call | solution.py:220
  17.2 0.6 %copy.7 = bf16[2,32,128]{2,1,0:T(8,128)(2,1)} copy(bf16[2,32,128]{2,1,0:T(8,128)(2,1)S(1)} %bitcast.3) | data formatting | bytes 32768

commit v4 on v3

v4 whole, which is shorter than its diff:
```python
import functools

import jax
import jax.numpy as jnp
from jax import lax
from jax.experimental import pallas as pl
from jax.experimental.pallas import tpu as pltpu
from jax.sharding import PartitionSpec as P

MESH = pl.DeviceIdType.MESH
CHUNK = 512
WAVE = 2
MXU = False
UNROLL = 1
FOUR = 4
GROUP_BYTES = 1 << 20


def layer_norm(values, gain, axis):
    centered = values - jnp.mean(values, axis=axis, keepdims=True)
    variance = jnp.mean(centered * centered, axis=axis, keepdims=True)
    return centered * lax.rsqrt(variance + 1e-05) * gain


def one_side(normed, gate_weight, value_weight, pair_mask):
    both_weights = jnp.stack([gate_weight, value_weight])
    sides = jnp.einsum("rnd,qde->qern", normed, both_weights, preferred_element_type=jnp.float32)
    return (jax.nn.sigmoid(sides[0]) * sides[1] * pair_mask[None]).astype(jnp.bfloat16)


def send_sides(normed, weights, pair_mask):
    left_proj = one_side(normed, weights[0], weights[1], pair_mask)
    left_cols = lax.all_to_all(left_proj, "row", split_axis=0, concat_axis=1, tiled=True)
    right_proj = one_side(normed, weights[2], weights[3], pair_mask)
    right_cols = lax.all_to_all(right_proj, "row", split_axis=0, concat_axis=1, tiled=True)
    return (left_cols, right_cols)


def one_update(pair_now, pair_mask, weights, out_weight, gains, incoming):
    pair_f32 = pair_now.astype(jnp.float32)
    normed = layer_norm(pair_f32, gains[0], -1).astype(jnp.bfloat16)
    left_cols, right_cols = send_sides(normed, weights, pair_mask)
    gate_vals = jax.nn.sigmoid(
        jnp.einsum("rnd,de->rne", normed, weights[4], preferred_element_type=jnp.float32)
    )
    if incoming:
        triangle = jnp.einsum(
            "cki,ckj->cij", left_cols, right_cols, preferred_element_type=jnp.float32
        )
    else:
        triangle = jnp.einsum(
            "cik,cjk->cij", left_cols, right_cols, preferred_element_type=jnp.float32
        )
    own_rows = lax.all_to_all(
        triangle.astype(jnp.bfloat16), "row", split_axis=1, concat_axis=0, tiled=True
    ).astype(triangle.dtype)
    tri_normed = layer_norm(own_rows, gains[1][:, None, None], 0).astype(jnp.bfloat16)
    projected = jnp.einsum(
        "crn,ce->rne", tri_normed, out_weight, preferred_element_type=jnp.float32
    )
    return (pair_f32 + gate_vals * projected).astype(jnp.bfloat16)


def large_body(pair_rep, residue_mask, side_weights, out_weights, norm_gains):
    row_count = pair_rep.shape[0]
    first_row = lax.axis_index("row") * row_count
    mask_f32 = residue_mask.astype(jnp.float32)
    own_mask = lax.dynamic_slice_in_dim(mask_f32, first_row, row_count, 0)
    pair_mask = own_mask[:, None] * mask_f32[None, :]
    middle = one_update(pair_rep, pair_mask, side_weights[0], out_weights[0], norm_gains[0], False)
    return one_update(middle, pair_mask, side_weights[1], out_weights[1], norm_gains[1], True)


def waves(spans):
    return [list(range(begin, min(begin + WAVE, spans))) for begin in range(0, spans, WAVE)]


def mean_all(values, exact):
    chan = values.shape[1]
    high = values.astype(jnp.bfloat16)
    if exact:
        return dot(high, jnp.full((chan, chan), 1.0 / chan, jnp.bfloat16))
    low = (values - high.astype(jnp.float32)).astype(jnp.bfloat16)
    return dot(jnp.concatenate([high, low], axis=1), jnp.full((2 * chan, chan), 1.0 / chan, jnp.bfloat16))


def norm_rows(values, gain, exact):
    if not MXU:
        return layer_norm(values, gain, -1).astype(jnp.bfloat16)
    centered = values - mean_all(values, exact)
    variance = mean_all(centered * centered, False)
    return (centered * lax.rsqrt(variance + 1e-05) * gain).astype(jnp.bfloat16)


def sigmoid(values):
    return 0.5 * jnp.tanh(0.5 * values) + 0.5


def dot(a, b):
    return jnp.dot(a, b, preferred_element_type=jnp.float32)


def pair_kernel(
    ranks, size, rows,
    pair_ref, mask_ref, side_ref, out_ref, gain_ref, result_ref,
    pair_half, side_w, out_w, gain_w, mask_w, mask_col,
    right_put, right_got, mid_put, mid_got, left_put, left_got,
    pair_mask, left, gate, tri, pair_mid, normed_mid, right_mid, right_t,
    send_sem, recv_sem, pass_sem, take_sem, load_sem,
):
    chan = pair_half.shape[1]
    block = rows * size
    half = pair_half.shape[0]
    depth = half // size
    grp, me = lax.axis_index("grp"), lax.axis_index("row")
    spans = ranks // 4
    here, core = me // 4, me % 2
    slot, sibling = me // 2, me + 1 - 2 * (me % 2)
    beside = slot + 1 - 2 * (slot % 2)

    def slots_of(step):
        first = (here + step) % spans * 2
        return [first + slot % 2, first + beside % 2]

    direct = [slots_of(step) for step in range(spans)]
    direct[0] = direct[0][1:]
    peers = direct[0] + [peer for step in range(spans - 1, 0, -1) for peer in direct[step]]

    barrier = pltpu.get_barrier_semaphore()
    for rank in [2 * peer + core for peer in peers] + [sibling]:
        pl.semaphore_signal(barrier, inc=1, device_id=(grp, rank), device_id_type=MESH)

    def part(at):
        return pair_half.at[pl.ds(pl.multiple_of(at * block, block), block)]

    loads = [
        pltpu.make_async_copy(source, target, load_sem.at[index])
        for index, (source, target) in enumerate(
            [(pair_ref, part(slot)), (mask_ref, mask_w), (side_ref, side_w), (out_ref, out_w), (gain_ref, gain_w)]
        )
    ]
    for load in loads:
        load.start()

    loads[1].wait()
    at_row = lax.broadcasted_iota(jnp.int32, (size, size), 0)
    at_col = lax.broadcasted_iota(jnp.int32, (size, size), 1)
    mask_row = jnp.broadcast_to(mask_w[...].astype(jnp.float32), (size, size))
    column = jnp.sum(jnp.where(at_row == at_col, mask_row, 0.0), axis=1, keepdims=True)
    mask_col[...] = jnp.broadcast_to(column, (size, chan))

    pl.semaphore_wait(barrier, len(peers) + 1)

    copies = []
    for index, peer in enumerate(peers):
        copies.append(pltpu.make_async_remote_copy(
            src_ref=pair_ref, dst_ref=part(slot), send_sem=send_sem.at[index],
            recv_sem=recv_sem.at[slot], device_id=(grp, 2 * peer + core), device_id_type=MESH,
        ))
        copies[-1].start()

    def arrive(at):
        pltpu.make_async_remote_copy(
            src_ref=part(at), dst_ref=part(at), send_sem=send_sem.at[0],
            recv_sem=recv_sem.at[at], device_id=(grp, sibling), device_id_type=MESH,
        ).wait_recv()

    def swap(source, target, index):
        copy = pltpu.make_async_remote_copy(
            src_ref=source, dst_ref=target, send_sem=pass_sem.at[index],
            recv_sem=take_sem.at[index], device_id=(grp, sibling), device_id_type=MESH,
        )
        copy.start()
        copies.append(copy)
        return copy

    def fill_mask(at, carry):
        first = at // rows * 2 * rows + core * rows + at % rows
        mask_one = mask_col[pl.ds(first, 1), :]
        pair_mask[pl.ds(pl.multiple_of(at * size, size), size), :] = mask_one * mask_col[...]
        return carry

    lax.fori_loop(0, depth, fill_mask, 0)

    for load in (loads[0], loads[2], loads[3], loads[4]):
        load.wait()

    gains = [[gain_w[u, pl.ds(q, 1), :] for q in range(2)] for u in range(2)]
    chunk = 2 * block

    def spread(values, first, parity):
        for index in range(chunk // size):
            at = first // size // rows * 2 * rows + (index // rows * 2 + parity) * rows + index % rows
            right_t[pl.ds(at, size, stride=size), :] = values[index * size:(index + 1) * size]

    def project(firsts):
        values = jnp.concatenate([pair_half[pl.ds(first, chunk), :] for first in firsts], axis=0)
        normed = norm_rows(values.astype(jnp.float32), gains[0][0], True)
        mask = jnp.concatenate([pair_mask[pl.ds(first, chunk), :] for first in firsts], axis=0)
        rights = dot(normed, jnp.concatenate([side_w[0, 2], side_w[0, 3]], axis=1))
        rights = (sigmoid(rights[:, :chan]) * rights[:, chan:] * mask).astype(jnp.bfloat16)
        for at, first in enumerate(firsts):
            right_put[pl.ds(first, chunk), :] = rights[at * chunk:(at + 1) * chunk]
        rights = rights.astype(jnp.float32)
        lefts = dot(normed, jnp.concatenate([side_w[0, 0], side_w[0, 1]], axis=1))
        lefts = (sigmoid(lefts[:, :chan]) * lefts[:, chan:] * mask).astype(jnp.bfloat16).astype(jnp.float32)
        gates = sigmoid(dot(normed, side_w[0, 4]))
        for at, first in enumerate(firsts):
            rows_at = slice(at * chunk, (at + 1) * chunk)
            left[pl.ds(first, chunk), :] = lefts[rows_at]
            gate[pl.ds(first, chunk), :] = gates[rows_at]
            spread(rights[rows_at], first, core)

    swaps = []
    for steps in waves(spans):
        for step in steps:
            for at in direct[step]:
                arrive(at)
        firsts = [pl.multiple_of((here + step) % spans * chunk, chunk) for step in steps]
        project(firsts)
        for first, step in zip(firsts, steps):
            span = pl.ds(first, chunk)
            swaps.append(swap(right_put.at[span], right_got.at[span], step))
    for step in range(spans):
        swaps[step].wait_recv()
        first = pl.multiple_of((here + step) % spans * chunk, chunk)
        spread(right_got[pl.ds(first, chunk), :].astype(jnp.float32), first, 1 - core)

    def outgoing(step, carry):
        first = pl.multiple_of(step * 4 * size, 4 * size)
        sums = [jnp.zeros((size, chan), jnp.float32) for _ in range(4)]
        for k in range(size):
            rights = right_t[k * size:(k + 1) * size, :]
            for index in range(4):
                sums[index] += left[pl.ds(first + index * size + k, 1), :] * rights
        for index in range(4):
            tri[pl.ds(pl.multiple_of(first + index * size, size), size), :] = sums[index]
        return carry

    lax.fori_loop(0, depth // 4, outgoing, 0)

    swaps = []
    for begin in range(0, half, CHUNK):
        span = slice(begin, begin + CHUNK)
        tri_normed = norm_rows(tri[span, :], gains[0][1], False)
        middle = pair_half[span, :].astype(jnp.float32) + gate[span, :] * dot(tri_normed, out_w[0])
        middle = middle.astype(jnp.bfloat16).astype(jnp.float32)
        pair_mid[span, :] = middle
        normed = norm_rows(middle, gains[1][0], True)
        normed_mid[span, :] = normed.astype(jnp.float32)
        rights = dot(normed, jnp.concatenate([side_w[1, 2], side_w[1, 3]], axis=1))
        rights = (sigmoid(rights[:, :chan]) * rights[:, chan:] * pair_mask[span, :]).astype(jnp.bfloat16)
        mid_put[span, :] = rights
        swaps.append(swap(mid_put.at[span], mid_got.at[span], spans + begin // CHUNK))
        right_mid[span, :] = rights.astype(jnp.float32)

    wanted = [pl.ds(rank * rows + index, depth, stride=size) for rank in (sibling, me) for index in range(rows)]
    columns = jnp.concatenate([normed_mid[at, :] for at in wanted], axis=0).astype(jnp.bfloat16)
    column_mask = jnp.concatenate([pair_mask[at, :] for at in wanted], axis=0)
    lefts = dot(columns, jnp.concatenate([side_w[1, 0], side_w[1, 1]], axis=1))
    lefts = (sigmoid(lefts[:, :chan]) * lefts[:, chan:] * column_mask).astype(jnp.bfloat16)
    left_put[...] = lefts[:rows * depth]
    swaps.append(swap(left_put, left_got, spans + half // CHUNK))
    left_own = lefts[rows * depth:].astype(jnp.float32)

    own = pl.ds(pl.multiple_of(slot * block, block), block)
    gate_own = sigmoid(dot(normed_mid[own, :].astype(jnp.bfloat16), side_w[1, 4]))
    sums = [jnp.zeros((size, chan), jnp.float32) for _ in range(rows)]
    for k in range(depth):
        rights = right_mid[k * size:(k + 1) * size, :]
        for index in range(rows):
            sums[index] += left_own[index * depth + k:index * depth + k + 1] * rights
    for copy in swaps:
        copy.wait_recv()
    left_own = left_got[...].astype(jnp.float32)
    for k in range(depth):
        rights = mid_got[k * size:(k + 1) * size, :].astype(jnp.float32)
        for index in range(rows):
            sums[index] += left_own[index * depth + k:index * depth + k + 1] * rights
    tri_normed = norm_rows(jnp.concatenate(sums, axis=0), gains[1][1], False)
    result_ref[...] = (pair_mid[own, :] + gate_own * dot(tri_normed, out_w[1])).astype(jnp.bfloat16)

    for copy in copies:
        copy.wait_send()


def group_body(ranks, pair_rep, residue_mask, side_weights, out_weights, norm_gains):
    rows, size, chan = pair_rep.shape
    half = size * size // 2
    narrow, wide = pltpu.VMEM((half, chan), jnp.bfloat16), pltpu.VMEM((half, chan), jnp.float32)
    edge = pltpu.VMEM((rows * size // 2, chan), jnp.bfloat16)
    swaps = ranks // 4 + half // CHUNK + 1
    result = pl.pallas_call(
        functools.partial(pair_kernel, ranks, size, rows),
        out_shape=pltpu.VMEM((rows * size, chan), jnp.bfloat16),
        in_specs=[pl.BlockSpec(memory_space=pltpu.HBM)] * 5,
        out_specs=pl.BlockSpec(memory_space=pltpu.VMEM),
        scratch_shapes=[
            narrow,
            pltpu.VMEM(side_weights.shape, jnp.bfloat16),
            pltpu.VMEM(out_weights.shape, jnp.bfloat16),
            pltpu.VMEM(norm_gains.shape, jnp.float32),
            pltpu.VMEM((1, size), jnp.int32),
            pltpu.VMEM((size, chan), jnp.float32),
            narrow, narrow, narrow, narrow, edge, edge,
            wide, wide, wide, wide, wide, wide, wide,
            pltpu.VMEM((2 * half, chan), jnp.float32),
            pltpu.SemaphoreType.DMA((ranks // 2,)),
            pltpu.SemaphoreType.DMA((ranks // 2,)),
            pltpu.SemaphoreType.DMA((swaps,)),
            pltpu.SemaphoreType.DMA((swaps,)),
            pltpu.SemaphoreType.DMA((5,)),
        ],
        compiler_params=pltpu.CompilerParams(
            collective_id=0, has_side_effects=True, vmem_limit_bytes=60 << 20
        ),
    )(pair_rep.reshape(rows * size, chan), residue_mask.reshape(1, size), side_weights, out_weights, norm_gains)
    return result.reshape(pair_rep.shape)


def body(ranks, pair_rep, residue_mask, side_weights, out_weights, norm_gains):
    rows, size, chan = pair_rep.shape
    fits = size * size * chan * 4 <= GROUP_BYTES and size * size // 2 % CHUNK == 0 and rows * ranks == size and size % 16 == 0
    if fits and ranks % 4 == 0 and ranks > 4:
        return group_body(ranks, pair_rep, residue_mask, side_weights, out_weights, norm_gains)
    return large_body(pair_rep, residue_mask, side_weights, out_weights, norm_gains)


def solution(mesh):
    in_specs = (P(("grp", "row"), None, None), P("grp"), P(), P(), P())
    out_specs = P(("grp", "row"), None, None)
    mapped = functools.partial(body, mesh.shape["row"])
    return jax.shard_map(mapped, mesh=mesh, in_specs=in_specs, out_specs=out_specs, check_vma=False)
```

time: 17.9 us -> 15.8 us (0.88)
  the two profiles are of different devices: /device:TPU:1 before, /device:TPU:0 now
where the time goes in v4:
time: 15.8 us; the launch traced here: 15.7 us
  Pallas kernels  15 us (95%)
  local copies, waits for them, and re-layouts  0.61 us (4%)
    pallas_call x1, Pallas kernels, group_body(): pl.pallas_call(functools.partial(pair_kernel, ranks, size, rows), out_sha...  15 us
    unnamed x1, local copies, waits for them, and re-layouts  0.61 us

profile of v4, /device:TPU:0, one launch (start us, length us, event | category | flops | bytes accessed | tf_op | source)
XLA Modules:
  0.0 15.7 jit_solution(2345375348212097555)
XLA Ops:
  0.0 15.0 %shard_map.55 = bf16[64,128]{1,0:T(8,128)(2,1)S(1)} custom-call(bf16[64,128]{1,0:T(8,128)(2,1)} %bitcast.4, s32[1,32]{1,0:T(1,128)} %bitcast.5, bf16[2,5,128,128]{3,2,1,0:T(8,128)(2,1)} %side_ref.1, bf16[2,128,128]{2,1,0:T(8,128)(2,1)} %out_ref.1, f32[2,2,128]{2,1,0:T(2,128)} %gain_ref.1), custom_call_target="tpu_custom_call" | custom-call | tf_op jit(solution)/shard_map/pallas_call | solution.py:293
  15.1 0.6 %copy.7 = bf16[2,32,128]{2,1,0:T(8,128)(2,1)} copy(bf16[2,32,128]{2,1,0:T(8,128)(2,1)S(1)} %bitcast.3) | data formatting | bytes 32768

commit v5 on v4

--- a/solution.py
+++ b/solution.py
@@ -149,12 +149,13 @@
     column = jnp.sum(jnp.where(at_row == at_col, mask_row, 0.0), axis=1, keepdims=True)
     mask_col[...] = jnp.broadcast_to(column, (size, chan))
 
+    loads[0].wait()
     pl.semaphore_wait(barrier, len(peers) + 1)
 
     copies = []
     for index, peer in enumerate(peers):
         copies.append(pltpu.make_async_remote_copy(
-            src_ref=pair_ref, dst_ref=part(slot), send_sem=send_sem.at[index],
+            src_ref=part(slot), dst_ref=part(slot), send_sem=send_sem.at[index],
             recv_sem=recv_sem.at[slot], device_id=(grp, 2 * peer + core), device_id_type=MESH,
         ))
         copies[-1].start()
@@ -182,15 +183,15 @@
 
     lax.fori_loop(0, depth, fill_mask, 0)
 
-    for load in (loads[0], loads[2], loads[3], loads[4]):
+    for load in loads[2:]:
         load.wait()
 
     gains = [[gain_w[u, pl.ds(q, 1), :] for q in range(2)] for u in range(2)]
     chunk = 2 * block
 
-    def spread(values, first, parity):
+    def spread(values, first, turn):
         for index in range(chunk // size):
-            at = first // size // rows * 2 * rows + (index // rows * 2 + parity) * rows + index % rows
+            at = turn * depth + index % rows * (ranks // 2) + first // block + index // rows
             right_t[pl.ds(at, size, stride=size), :] = values[index * size:(index + 1) * size]
 
     def project(firsts):
@@ -209,7 +210,7 @@
             rows_at = slice(at * chunk, (at + 1) * chunk)
             left[pl.ds(first, chunk), :] = lefts[rows_at]
             gate[pl.ds(first, chunk), :] = gates[rows_at]
-            spread(rights[rows_at], first, core)
+            spread(rights[rows_at], first, 0)
 
     swaps = []
     for steps in waves(spans):
@@ -221,23 +222,27 @@
         for first, step in zip(firsts, steps):
             span = pl.ds(first, chunk)
             swaps.append(swap(right_put.at[span], right_got.at[span], step))
+    def outgoing(turn, step, carry):
+        first = pl.multiple_of(step * 8 * size, 8 * size)
+        sums = [jnp.zeros((depth, chan), jnp.float32) for _ in range(8)]
+        for k in range(size):
+            rights = right_t[k * size + turn * depth:k * size + (turn + 1) * depth, :]
+            for index in range(8):
+                sums[index] += left[pl.ds(first + index * size + k, 1), :] * rights
+        lead = core * rows if turn == 0 else (1 - core) * rows
+        count = ranks // 2
+        for index in range(8):
+            for row in range(rows):
+                at = first + index * size + lead + row
+                tri[pl.ds(at, count, stride=2 * rows), :] = sums[index][row * count:(row + 1) * count]
+        return carry
+
+    lax.fori_loop(0, depth // 8, functools.partial(outgoing, 0), 0, unroll=True)
     for step in range(spans):
         swaps[step].wait_recv()
         first = pl.multiple_of((here + step) % spans * chunk, chunk)
-        spread(right_got[pl.ds(first, chunk), :].astype(jnp.float32), first, 1 - core)
-
-    def outgoing(step, carry):
-        first = pl.multiple_of(step * 4 * size, 4 * size)
-        sums = [jnp.zeros((size, chan), jnp.float32) for _ in range(4)]
-        for k in range(size):
-            rights = right_t[k * size:(k + 1) * size, :]
-            for index in range(4):
-                sums[index] += left[pl.ds(first + index * size + k, 1), :] * rights
-        for index in range(4):
-            tri[pl.ds(pl.multiple_of(first + index * size, size), size), :] = sums[index]
-        return carry
-
-    lax.fori_loop(0, depth // 4, outgoing, 0)
+        spread(right_got[pl.ds(first, chunk), :].astype(jnp.float32), first, 1)
+    lax.fori_loop(0, depth // 8, functools.partial(outgoing, 1), 0, unroll=True)
 
     swaps = []
     for begin in range(0, half, CHUNK):

time: 15.8 us -> 15.1 us (0.956)
  Pallas kernels: 15 us -> 14.2 us
    pallas_call x1, Pallas kernels: 15 us -> 14.2 us  [group_body(): pl.pallas_call(functools.partial(pair_kernel, ranks, size, rows), out_sha...]
where the time goes in v5:
time: 15.1 us; the launch traced here: 14.9 us
  Pallas kernels  14.2 us (94%)
  local copies, waits for them, and re-layouts  0.61 us (4%)
    pallas_call x1, Pallas kernels, group_body(): pl.pallas_call(functools.partial(pair_kernel, ranks, size, rows), out_sha...  14.2 us
    unnamed x1, local copies, waits for them, and re-layouts  0.61 us

profile of v5, /device:TPU:0, one launch (start us, length us, event | category | flops | bytes accessed | tf_op | source)
XLA Modules:
  0.0 14.9 jit_solution(1162283676903316498)
XLA Ops:
  0.0 14.2 %shard_map.55 = bf16[64,128]{1,0:T(8,128)(2,1)S(1)} custom-call(bf16[64,128]{1,0:T(8,128)(2,1)} %bitcast.4, s32[1,32]{1,0:T(1,128)} %bitcast.5, bf16[2,5,128,128]{3,2,1,0:T(8,128)(2,1)} %side_ref.1, bf16[2,128,128]{2,1,0:T(8,128)(2,1)} %out_ref.1, f32[2,2,128]{2,1,0:T(2,128)} %gain_ref.1), custom_call_target="tpu_custom_call" | custom-call | tf_op jit(solution)/shard_map/pallas_call | solution.py:298
  14.3 0.6 %copy.7 = bf16[2,32,128]{2,1,0:T(8,128)(2,1)} copy(bf16[2,32,128]{2,1,0:T(8,128)(2,1)S(1)} %bitcast.3) | data formatting | bytes 32768

commit v6 on v5

--- a/solution.py
+++ b/solution.py
@@ -11,8 +11,6 @@
 CHUNK = 512
 WAVE = 2
 MXU = False
-UNROLL = 1
-FOUR = 4
 GROUP_BYTES = 1 << 20
 
 
@@ -124,7 +122,7 @@
 
     direct = [slots_of(step) for step in range(spans)]
     direct[0] = direct[0][1:]
-    peers = direct[0] + [peer for step in range(spans - 1, 0, -1) for peer in direct[step]]
+    peers = direct[0] + [peer for step in range(1, spans) for peer in direct[step]]
 
     barrier = pltpu.get_barrier_semaphore()
     for rank in [2 * peer + core for peer in peers] + [sibling]:

time: 15.1 us -> 14.6 us (0.967)
  Pallas kernels: 14.2 us -> 13.8 us
    pallas_call x1, Pallas kernels: 14.2 us -> 13.8 us  [group_body(): pl.pallas_call(functools.partial(pair_kernel, ranks, size, rows), out_sha...]
where the time goes in v6:
time: 14.6 us; the launch traced here: 14.4 us
  Pallas kernels  13.8 us (95%)
  local copies, waits for them, and re-layouts  0.61 us (4%)
    pallas_call x1, Pallas kernels, group_body(): pl.pallas_call(functools.partial(pair_kernel, ranks, size, rows), out_sha...  13.8 us
    unnamed x1, local copies, waits for them, and re-layouts  0.61 us

profile of v6, /device:TPU:0, one launch (start us, length us, event | category | flops | bytes accessed | tf_op | source)
XLA Modules:
  0.0 14.4 jit_solution(7958624808185031837)
XLA Ops:
  0.0 13.8 %shard_map.55 = bf16[64,128]{1,0:T(8,128)(2,1)S(1)} custom-call(bf16[64,128]{1,0:T(8,128)(2,1)} %bitcast.4, s32[1,32]{1,0:T(1,128)} %bitcast.5, bf16[2,5,128,128]{3,2,1,0:T(8,128)(2,1)} %side_ref.1, bf16[2,128,128]{2,1,0:T(8,128)(2,1)} %out_ref.1, f32[2,2,128]{2,1,0:T(2,128)} %gain_ref.1), custom_call_target="tpu_custom_call" | custom-call | tf_op jit(solution)/shard_map/pallas_call | solution.py:296
  13.8 0.6 %copy.7 = bf16[2,32,128]{2,1,0:T(8,128)(2,1)} copy(bf16[2,32,128]{2,1,0:T(8,128)(2,1)S(1)} %bitcast.3) | data formatting | bytes 32768
